TPU v7x, 256 devices: a whole 4x4x8 slice. The times are simulated.
256 devices in a mesh: dp: 16 (over z, core), feat: 16 (over x, y).
Axes of the slice: x: 4, y: 4, z: 8, core: 2. Of those that a mesh axis runs over, the one named last changes fastest.
Arguments:
- design: bfloat16 [32768, 16384], P('dp', 'feat'), may hold values from -0.3314563 to 0.3314563
- sketch: bfloat16 [1536, 32768], P(None, 'dp'), may hold values from -0.15625 to 0.15625
- targets: float32 [64, 32768], P(None, 'dp'), may hold values from -6 to 6
Outputs:
- solution: float32 [64, 16384], P(None, 'feat')
- residual_ratio: float32 [64], replicated
All inputs are finite; a program needn't handle non-finite values.
Results may differ from a plain program's by a relative error of at most 0.0003.
Values sent between devices are 32-bit elements; how exact they have to be, the bound alone decides.
A program may use at most 128 MiB of HBM per device.

v0:
```python
import jax
import jax.numpy as jnp
from jax import lax
from jax.sharding import PartitionSpec as P

ITERS = 2


NORM_EPS = 1e-06
TOP_PRECISION = lax.Precision.HIGHEST


def body(design, sketch, targets):
    block_cols = design.shape[1]
    target_count = targets.shape[0]
    sketched = lax.psum_scatter(
        jnp.dot(sketch, design, preferred_element_type=jnp.float32),
        "dp",
        scatter_dimension=0,
        tiled=True,
    )
    local_gram = jnp.dot(
        sketched.T, sketched, precision=TOP_PRECISION, preferred_element_type=jnp.float32
    )
    gram_mat = lax.psum(local_gram, "dp")
    low_factor = jnp.linalg.cholesky(gram_mat)

    def precondition(vec):
        return lax.linalg.triangular_solve(low_factor, vec, left_side=False, lower=True)

    def adjoint_pre(vec):
        return lax.linalg.triangular_solve(
            low_factor, vec, left_side=False, lower=True, transpose_a=True
        )

    def adjoint_local(vec):
        return jnp.dot(vec, design, precision=TOP_PRECISION, preferred_element_type=jnp.float32)

    def squares_of(vec):
        return jnp.sum(vec * vec, axis=1)

    coords = jnp.zeros((target_count, block_cols), jnp.float32)

    def row_norm(vec):
        return jnp.sqrt(lax.psum(squares_of(vec), "dp") + NORM_EPS)

    def col_norm(vec):
        return jnp.sqrt(lax.psum(squares_of(vec), "feat") + NORM_EPS)

    def adjoint_sum(vec):
        return adjoint_pre(lax.psum(adjoint_local(vec), "dp"))

    beta_norm = row_norm(targets)
    beta_first = beta_norm
    left_vec = targets / beta_norm[:, None]
    right_raw = adjoint_sum(left_vec)
    alpha_norm = col_norm(right_raw)
    right_vec = right_raw / alpha_norm[:, None]
    search_dir = right_vec
    rho_bar = alpha_norm
    phi_bar = beta_norm
    for step_idx in range(ITERS):
        image_rows = lax.psum(
            jnp.dot(
                precondition(right_vec),
                design.T,
                precision=TOP_PRECISION,
                preferred_element_type=jnp.float32,
            ),
            "feat",
        )
        left_raw = image_rows - alpha_norm[:, None] * left_vec
        beta_norm = row_norm(left_raw)
        left_vec = left_raw / beta_norm[:, None]
        rho_full = jnp.sqrt(rho_bar * rho_bar + beta_norm * beta_norm)
        cosine = rho_bar / rho_full
        sine_val = beta_norm / rho_full
        phi_step = cosine * phi_bar
        phi_bar = sine_val * phi_bar
        coords = coords + (phi_step / rho_full)[:, None] * search_dir
        if step_idx + 1 < ITERS:
            right_raw = adjoint_sum(left_vec) - beta_norm[:, None] * right_vec
            alpha_norm = col_norm(right_raw)
            right_vec = right_raw / alpha_norm[:, None]
            theta_val = sine_val * alpha_norm
            rho_bar = -cosine * alpha_norm
            search_dir = right_vec - (theta_val / rho_full)[:, None] * search_dir
    return (precondition(coords), phi_bar / beta_first)


def solution(mesh):
    return jax.shard_map(
        body,
        mesh=mesh,
        in_specs=(P("dp", "feat"), P(None, "dp"), P(None, "dp")),
        out_specs=(P(None, "feat"), P()),
        check_vma=False,
    )
```

profile of v0, /device:TPU:1, one launch (start us, length us, event | category | flops | bytes accessed | tf_op | source)
XLA Modules:
  0.0 1040.0 jit_solution(5861815129539548095)
XLA Ops:
  7.2 11.7 %fusion.200 = f32[1536,1024]{1,0:T(8,128)} fusion(bf16[1536,2048]{1,0:T(8,128)(2,1)} %param.8, bf16[2048,1024]{1,0:T(8,128)(2,1)} %param.7), kind=kOutput, calls=%fused_computation.447 | convolution fusion | flops 6442450944 | bytes 16777216 | tf_op jit(solution)/shard_map/dot_general | solution.py:17
  20.0 27.6 %psum.71 = f32[64]{0:T(128)S(1)} all-reduce(f32[64]{0:T(128)S(1)} %multiply_reduce_fusion.2), channel_id=1, replica_groups=mesh['dp'=16,'feat'=16] {'dp'}, use_global_device_ids=true, to_apply=%region_19.20 | all-reduce | flops 64 | bytes 512 | tf_op jit(solution)/shard_map/psum | solution.py:45
  47.6 5.3 fusion.109
  52.9 33.5 %reduce-scatter.2.cloned.1.call-done = f32[96,1024]{1,0:T(8,128)} async-done(((f32[1536,1024]{1,0:T(8,128)}), f32[96,1024]{1,0:T(8,128)}) %reduce-scatter.2.cloned.1.call-update) | async-done | bytes 393232 | tf_op jit(solution)/shard_map/reduce_scatter | solution.py:16
  86.4 6.5 fusion.201
  93.1 123.9 %all-reduce.13.cloned.1.call-done = (f32[1024,1024]{0,1:T(8,128)}, f32[64,1024]{1,0:T(8,128)}) async-done(((f32[1024,1024]{0,1:T(8,128)}, f32[64,1024]{1,0:T(8,128)}), (f32[1024,1024]{0,1:T(8,128)}, f32[64,1024]{1,0:T(8,128)})) %all-reduce.13.cloned.1.call-update) | async-done | bytes 4456464 | tf_op jit(solution)/shard_map/psum | solution.py:25
  216.9 5.5 copy.6
  222.5 4.4 fusion
  228.9 11.7 %cholesky.223 = f32[128,128]{1,0:T(8,128)S(1)} custom-call(f32[128,128]{1,0:T(8,128)S(1)} %cholesky.580), custom_call_target="Cholesky" | custom-call | tf_op jit(solution)/shard_map/jit(cholesky)/cholesky | solution.py:26
  240.6 9.8 custom-call.65
  250.5 2.5 cholesky.255
  252.9 2.4 constant_dynamic-update-slice_fusion.132
  256.9 11.9 %cholesky.244 = f32[128,128]{1,0:T(8,128)S(1)} custom-call(f32[128,128]{1,0:T(8,128)S(1)} %cholesky.584), custom_call_target="Cholesky" | custom-call | tf_op jit(solution)/shard_map/jit(cholesky)/cholesky | solution.py:26
  269.4 9.8 custom-call.66
  282.6 11.7 %cholesky.468 = f32[128,128]{1,0:T(8,128)S(1)} custom-call(f32[128,128]{1,0:T(8,128)S(1)} %cholesky.589), custom_call_target="Cholesky" | custom-call | tf_op jit(solution)/shard_map/jit(cholesky)/cholesky | solution.py:26
  295.6 9.8 custom-call.67
  306.6 2.3 convolution_subtract_fusion.2
  309.0 12.1 %cholesky.487 = f32[128,128]{1,0:T(8,128)S(1)} custom-call(f32[128,128]{1,0:T(8,128)S(1)} %cholesky.594), custom_call_target="Cholesky" | custom-call | tf_op jit(solution)/shard_map/jit(cholesky)/cholesky | solution.py:26
  322.3 9.8 custom-call.68
  333.3 2.3 convolution_subtract_fusion.3
  335.6 11.7 %cholesky.506 = f32[128,128]{1,0:T(8,128)S(1)} custom-call(f32[128,128]{1,0:T(8,128)S(1)} %cholesky.599), custom_call_target="Cholesky" | custom-call | tf_op jit(solution)/shard_map/jit(cholesky)/cholesky | solution.py:26
  348.6 9.9 custom-call.69
  359.5 2.3 convolution_subtract_fusion.4
  361.8 11.7 %cholesky.526 = f32[128,128]{1,0:T(8,128)S(1)} custom-call(f32[128,128]{1,0:T(8,128)S(1)} %cholesky.604), custom_call_target="Cholesky" | custom-call | tf_op jit(solution)/shard_map/jit(cholesky)/cholesky | solution.py:26
  374.8 9.8 custom-call.70
  387.6 11.9 %cholesky.546 = f32[128,128]{1,0:T(8,128)S(1)} custom-call(f32[128,128]{1,0:T(8,128)S(1)} %cholesky.609), custom_call_target="Cholesky" | custom-call | tf_op jit(solution)/shard_map/jit(cholesky)/cholesky | solution.py:26
  400.8 9.8 custom-call.71
  413.4 11.7 %cholesky.564 = f32[128,128]{1,0:T(8,128)S(1)} custom-call(f32[128,128]{1,0:T(8,128)S(1)} %convolution_subtract_fusion.6), custom_call_target="Cholesky" | custom-call | tf_op jit(solution)/shard_map/jit(cholesky)/cholesky | solution.py:26
  432.0 4.9 select_select_fusion
  436.9 23.4 %while.10 = (s32[]{:T(128)}, f32[1024,1024]{1,0:T(8,128)}, s32[8,2]{0,1:T(2,128)S(1)}, f32[8,128,128]{2,1,0:T(8,128)S(1)}, s32[]{:T(128)}) while((s32[]{:T(128)}, f32[1024,1024]{1,0:T(8,128)}, s32[8,2]{0,1:T(2,128)S(1)}, f32[8,128,128]{2,1,0:T(8,128)S(1)}, s32[]{:T(128)}) %tuple.114), condition=%wide.while_cond, body=%wide.while_body.sunk | while | flops 2 | bytes 131181 | solution.py:32
  437.5 2.3 bitcast_dynamic-update-slice_fusion.2
  440.5 2.3 bitcast_dynamic-update-slice_fusion.2
  443.4 2.3 bitcast_dynamic-update-slice_fusion.2
  446.3 2.3 bitcast_dynamic-update-slice_fusion.2
  449.3 2.3 bitcast_dynamic-update-slice_fusion.2
  452.2 2.3 bitcast_dynamic-update-slice_fusion.2
  455.2 2.3 bitcast_dynamic-update-slice_fusion.2
  460.3 79.0 %custom-call.75 = f32[8,128,128]{1,2,0:T(8,128)S(1)} custom-call(f32[8,128,128]{2,1,0:T(8,128)S(1)} %get-tuple-element.38), custom_call_target="InvertDiagBlocksLowerTriangular" | custom-call | tf_op jit(solution)/shard_map/triangular_solve/custom-call.7 | solution.py:32
  550.6 33.1 %psum.73 = f32[64]{0:T(128)S(1)} all-reduce(f32[64]{0:T(128)S(1)} %multiply_reduce_fusion.4), channel_id=1, replica_groups=mesh['dp'=16,'feat'=16] {'feat'}, use_global_device_ids=true, to_apply=%region_22.24 | all-reduce | flops 64 | bytes 512 | tf_op jit(solution)/shard_map/psum | solution.py:48
  594.9 4.7 fusion.202
  599.7 97.0 %all-reduce.7.cloned.1.call-done = f32[64,2048]{1,0:T(8,128)} async-done(((f32[64,2048]{1,0:T(8,128)}), f32[64,2048]{1,0:T(8,128)}) %all-reduce.7.cloned.1.call-update) | async-done | bytes 524304 | tf_op jit(solution)/shard_map/psum | solution.py:63
  698.1 25.4 %psum.75 = f32[64]{0:T(128)S(1)} all-reduce(f32[64]{0:T(128)S(1)} %get-tuple-element.57), channel_id=1, replica_groups=mesh['dp'=16,'feat'=16] {'dp'}, use_global_device_ids=true, to_apply=%region_25.28 | all-reduce | flops 64 | bytes 512 | tf_op jit(solution)/shard_map/psum | solution.py:45
  723.4 5.3 fusion.110
  728.9 107.2 %all-reduce.9.cloned.1.call-done = f32[64,1024]{1,0:T(8,128)} async-done(((f32[64,1024]{1,0:T(8,128)}), f32[64,1024]{1,0:T(8,128)}) %all-reduce.9.cloned.1.call-update) | async-done | bytes 262160 | tf_op jit(solution)/shard_map/psum | solution.py:51
  848.3 33.1 %psum.77 = f32[64]{0:T(128)S(1)} all-reduce(f32[64]{0:T(128)S(1)} %multiply_reduce_fusion.3), channel_id=1, replica_groups=mesh['dp'=16,'feat'=16] {'feat'}, use_global_device_ids=true, to_apply=%region_28.31 | all-reduce | flops 64 | bytes 512 | tf_op jit(solution)/shard_map/psum | solution.py:48
  892.7 4.7 fusion.203
  897.4 96.9 %all-reduce.11.cloned.1.call-done = f32[64,2048]{1,0:T(8,128)} async-done(((f32[64,2048]{1,0:T(8,128)}), f32[64,2048]{1,0:T(8,128)}) %all-reduce.11.cloned.1.call-update) | async-done | bytes 524304 | tf_op jit(solution)/shard_map/psum | solution.py:63
  995.6 25.4 %psum.79 = f32[64]{0:T(128)S(1)} all-reduce(f32[64]{0:T(128)S(1)} %multiply_reduce_fusion), channel_id=1, replica_groups=mesh['dp'=16,'feat'=16] {'dp'}, use_global_device_ids=true, to_apply=%region_31.34 | all-reduce | flops 64 | bytes 512 | tf_op jit(solution)/shard_map/psum | solution.py:45
  (229 shorter events, 94.0 us)
Async XLA Ops:
  7.2 79.3 %reduce-scatter.2.cloned.1.call-start = ((), (), s32[]{:S(2)}) async-start(), calls=%async_computation.1 | async-start | bytes 6684672 | tf_op jit(solution)/shard_map/reduce_scatter | solution.py:16
  18.9 1.0 copy-start.3
  18.9 198.1 %all-reduce.13.cloned.1.call-start = ((), (), s32[]{:S(2)}) async-start(), calls=%async_computation.5 | async-start | bytes 8912896 | tf_op jit(solution)/shard_map/psum | solution.py:25
  93.0 603.7 %all-reduce.7.cloned.1.call-start = ((), (), s32[]{:S(2)}) async-start(), calls=%async_computation.2 | async-start | bytes 1048576 | tf_op jit(solution)/shard_map/psum | solution.py:63
  226.9 2.0 copy-start.2
  432.0 107.3 %copy-start.4 = (f32[64,1024]{1,0:T(8,128)S(1)}, f32[64,1024]{1,0:T(8,128)}, u32[]{:S(2)}) copy-start(f32[64,1024]{1,0:T(8,128)} %get-tuple-element.52) | copy-start | bytes 786436
  583.7 11.3 %copy-start = (bf16[2048,1024]{1,0:T(8,128)(2,1)S(1)}, bf16[2048,1024]{1,0:T(8,128)(2,1)}, u32[]{:S(2)}) copy-start(bf16[2048,1024]{1,0:T(8,128)(2,1)} %param.7) | copy-start | bytes 12582916
  599.7 236.4 %all-reduce.9.cloned.1.call-start = ((), (), s32[]{:S(2)}) async-start(), calls=%async_computation.3 | async-start | bytes 524288 | tf_op jit(solution)/shard_map/psum | solution.py:51
  728.7 265.6 %all-reduce.11.cloned.1.call-start = ((), (), s32[]{:S(2)}) async-start(), calls=%async_computation.4 | async-start | bytes 1048576 | tf_op jit(solution)/shard_map/psum | solution.py:63
  881.4 11.3 %copy-start.1 = (bf16[2048,1024]{1,0:T(8,128)(2,1)S(1)}, bf16[2048,1024]{1,0:T(8,128)(2,1)}, u32[]{:S(2)}) copy-start(bf16[2048,1024]{1,0:T(8,128)(2,1)} %param.7) | copy-start | bytes 12582916
  1032.6 0.7 copy-start.5
Sparse Core Ops, SparseCore 0:
  19.0 67.3 reduce-scatter.1
  93.1 123.7 all-reduce.12
  599.8 96.8 all-reduce.6
  728.8 107.2 all-reduce.8
  897.5 96.7 all-reduce.10
where the time goes:
time: 1050 us; the launch traced here: 1040 us
  waiting for transfers between devices  459 us (44%)
  other arithmetic  265 us (25%)
  blocking collectives  144 us (14%)
  matrix products  116 us (11%)
  local copies, waits for them, and re-layouts  35.3 us (3%)
  between operations  20.1 us (2%)
    psum x2, waiting for transfers between devices, body(): lax.psum(jnp.dot(precondition(right_vec), design.T, precision=TOP_PRECISI...  194 us
    another operation x30, other arithmetic, body(): low_factor = jnp.linalg.cholesky(gram_mat)  172 us
    psum x1, waiting for transfers between devices, body(): gram_mat = lax.psum(local_gram, 'dp')  124 us
    psum x1, waiting for transfers between devices, adjoint_sum(): return adjoint_pre(lax.psum(adjoint_local(vec), 'dp'))  107 us
    another operation x4, other arithmetic, adjoint_pre(): lax.linalg.triangular_solve(low_factor, vec, left_side=False, lower=True,...  83.9 us
    psum x3, blocking collectives, row_norm(): return jnp.sqrt(lax.psum(squares_of(vec), 'dp') + NORM_EPS)  78.3 us
    psum x2, blocking collectives, col_norm(): return jnp.sqrt(lax.psum(squares_of(vec), 'feat') + NORM_EPS)  66.2 us
    reduce_scatter x1, waiting for transfers between devices, body(): lax.psum_scatter(jnp.dot(sketch, design, preferred_element_type=jnp.float...  33.5 us
  transfers between devices with their start and end apart: 5, of which 5 were waited for; matrix products, arithmetic and copies ran while one was open for 1% of the time, Pallas kernels for 0%

commit v1 on v0

v1 whole, which is shorter than its diff:
```python
import functools

import jax
import jax.numpy as jnp
from jax import lax
from jax.experimental import pallas as pl
from jax.experimental.pallas import tpu as pltpu
from jax.sharding import PartitionSpec as P

ITERS = 2
NORM_EPS = 1e-06
TOP_PRECISION = lax.Precision.HIGHEST
F32 = jnp.float32
BF16 = jnp.bfloat16
MESH = pl.DeviceIdType.MESH
NN = ((1,), (0,))
NT = ((1,), (1,))
SUB = 8
LANES = 128
BLK = 128
MIB = 2**20


def split3(x):
    high = x.astype(BF16)
    rest = x - high.astype(F32)
    mid = rest.astype(BF16)
    return high, mid, (rest - mid.astype(F32)).astype(BF16)


def dot32(a, b, dims):
    return lax.dot_general(a, b, (dims, ((), ())), preferred_element_type=F32)


def lane_splat(x, c):
    return jnp.broadcast_to(x[:, c : c + 1], x.shape)


def row_splat(x, r):
    return jnp.broadcast_to(x[r : r + 1, :], x.shape)


def tree_sum(terms):
    while len(terms) > 1:
        terms = [
            terms[i] + terms[i + 1] if i + 1 < len(terms) else terms[i]
            for i in range(0, len(terms), 2)
        ]
    return terms[0]


def factor_block(d_ref, w_ref):
    n = BLK // SUB
    rid = lax.broadcasted_iota(jnp.int32, (SUB, BLK), 0)
    lid = lax.broadcasted_iota(jnp.int32, (SUB, BLK), 1)
    a = [d_ref[SUB * i : SUB * i + SUB, :] for i in range(n)]
    w = [jnp.where(lid == rid + SUB * i, 1.0, 0.0) for i in range(n)]
    for g in range(n):
        cols = [lane_splat(a[g], SUB * g + c) for c in range(SUB)]
        rows_a, rows_w, low_w = a[g], w[g], w[g]
        inv_pivots = jnp.zeros((SUB, BLK), F32)
        for k in range(SUB):
            inv = 1.0 / row_splat(cols[k], k)
            mult = jnp.where(rid == k, 0.0, cols[k]) * inv
            for j in range(k + 1, SUB):
                cols[j] = cols[j] - mult * row_splat(cols[j], k)
            rows_a = rows_a - mult * row_splat(rows_a, k)
            rows_w = rows_w - mult * row_splat(rows_w, k)
            low_w = low_w - jnp.where(rid > k, mult, 0.0) * row_splat(low_w, k)
            inv_pivots = jnp.where(rid == k, inv, inv_pivots)
        rows_a = rows_a * inv_pivots
        rows_w = rows_w * inv_pivots
        w_ref[SUB * g : SUB * g + SUB, :] = low_w * jnp.sqrt(inv_pivots)
        if g < n - 1:
            splat_a = [row_splat(rows_a, c) for c in range(SUB)]
            splat_w = [row_splat(rows_w, c) for c in range(SUB)]
            for i in range(g + 1, n):
                p = [lane_splat(a[i], SUB * g + c) for c in range(SUB)]
                a[i] = a[i] - tree_sum([p[c] * splat_a[c] for c in range(SUB)])
                w[i] = w[i] - tree_sum([p[c] * splat_w[c] for c in range(SUB)])


def factor_kernel(g_in, w_ref, g_ref, d_ref, wk_ref, x_ref, y_ref, z_ref):
    size = g_ref.shape[0]
    blocks = size // BLK
    g_ref[...] = g_in[...]
    w_ref[...] = jnp.zeros_like(w_ref)

    def step(k, carry):
        at = pl.multiple_of(k * BLK, BLK)
        d_ref[...] = g_ref[pl.ds(at, BLK), pl.ds(at, BLK)]
        factor_block(d_ref, wk_ref)
        for this in range(blocks):

            @pl.when(k == this)
            def _():
                lo = this * BLK
                nxt = lo + BLK
                wk = wk_ref[...]
                wh, wm, wl = split3(wk)
                if this > 0:
                    ah, am, al = split3(w_ref[lo:nxt, 0:lo])
                    row = dot32(
                        jnp.concatenate([wh, wh, wm, wh, wm, wl], axis=1),
                        jnp.concatenate([ah, am, ah, al, am, ah], axis=0),
                        NN,
                    )
                    w_ref[lo:nxt, 0:lo] = row
                    rh, rm, rl = split3(row)
                    for t, part in enumerate([rh, rm, rh, rl, rm, rh]):
                        z_ref[t * BLK : (t + 1) * BLK, 0:lo] = part
                w_ref[lo:nxt, lo:nxt] = wk
                for t, part in enumerate([wh, wm, wh, wl, wm, wh]):
                    z_ref[t * BLK : (t + 1) * BLK, lo:nxt] = part
                if nxt < size:
                    gh, gm, gl = split3(g_ref[nxt:, lo:nxt])
                    panel = dot32(
                        jnp.concatenate([gh, gh, gm, gh, gm, gl], axis=1),
                        jnp.concatenate([wh, wm, wh, wl, wm, wh], axis=1),
                        NT,
                    )
                    ph, pm, pw = split3(panel)
                    for t, part in enumerate([ph, ph, pm, ph, pm, pw]):
                        x_ref[nxt:, t * BLK : (t + 1) * BLK] = part
                    for t, part in enumerate([ph, pm, ph, pw, pm, ph]):
                        y_ref[nxt:, t * BLK : (t + 1) * BLK] = part
                    j = nxt
                    while j < size:
                        wide = 2 * BLK if j % (2 * BLK) == 0 else BLK
                        g_ref[j:, j : j + wide] -= dot32(x_ref[j:, :], y_ref[j : j + wide, :], NT)
                        j += wide
                    w_ref[nxt:, 0:nxt] -= dot32(x_ref[nxt:, :], z_ref[:, 0:nxt], NN)

        return carry

    lax.fori_loop(0, blocks, step, 0)


def inverse_factor(gram):
    size = gram.shape[0]
    return pl.pallas_call(
        factor_kernel,
        out_shape=jax.ShapeDtypeStruct((size, size), F32),
        in_specs=[pl.BlockSpec(memory_space=pltpu.VMEM)],
        out_specs=pl.BlockSpec(memory_space=pltpu.VMEM),
        scratch_shapes=[
            pltpu.VMEM((size, size), F32),
            pltpu.VMEM((BLK, BLK), F32),
            pltpu.VMEM((BLK, BLK), F32),
            pltpu.VMEM((size, 6 * BLK), BF16),
            pltpu.VMEM((size, 6 * BLK), BF16),
            pltpu.VMEM((6 * BLK, size), BF16),
        ],
        compiler_params=pltpu.CompilerParams(vmem_limit_bytes=48 * MIB),
    )(gram)


class Group:
    def __init__(self, axis, n):
        self.axis, self.n = axis, n
        self.me = lax.axis_index(axis)

    def peer(self, t):
        return lax.rem(self.me + t, self.n)

    def source(self, t):
        return lax.rem(self.me + self.n - t, self.n)

    def each(self, fn):
        def step(t, carry):
            fn(t)
            return carry

        lax.fori_loop(1, self.n, step, 0)

    def copy(self, src, dst, sems, t):
        return pltpu.make_async_remote_copy(
            src_ref=src,
            dst_ref=dst,
            send_sem=sems.at[0, t - 1],
            recv_sem=sems.at[1, t - 1],
            device_id={self.axis: self.peer(t)},
            device_id_type=MESH,
        )

    def greet(self, barrier):
        self.each(
            lambda t: pl.semaphore_signal(
                barrier, inc=1, device_id={self.axis: self.peer(t)}, device_id_type=MESH
            )
        )

    def scatter_sum(self, stage, recv, sems):
        self.each(lambda t: self.copy(stage.at[self.peer(t)], recv.at[t - 1], sems, t).start())
        self.each(lambda t: self.copy(stage.at[self.peer(t)], recv.at[t - 1], sems, t).wait())
        return tree_sum([stage[self.me]] + [recv[t] for t in range(self.n - 1)])

    def gather(self, value, out, sems):
        out[self.me] = value
        self.each(lambda t: self.copy(out.at[self.me], out.at[self.me], sems, t).start())

        def wait(t):
            src = self.source(t)
            self.copy(out.at[src], out.at[src], sems, t).wait_recv()
            self.copy(out.at[self.me], out.at[self.me], sems, t).wait_send()

        self.each(wait)


def lane_partial(x):
    return tree_sum(
        [x[:, i : i + LANES] * x[:, i : i + LANES] for i in range(0, x.shape[1], LANES)]
    )


def norm_of(lanes):
    return jnp.sqrt(jnp.sum(lanes, axis=1, keepdims=True) + NORM_EPS)


def put_slices(stage, value, extra):
    n, _, wide = stage.shape
    halves = n * SUB // value.shape[0]
    part = value.shape[1] // halves
    for d in range(n):
        r, h = SUB * (d // halves), part * (d % halves)
        stage[d, :, 0:part] = value[r : r + SUB, h : h + part]
        if extra is not None:
            stage[d, :, part:wide] = extra[r : r + SUB, :]


def take_slices(out, k, part):
    n = out.shape[0]
    halves = n * SUB // k
    value = jnp.concatenate(
        [
            jnp.concatenate([out[g * halves + h, :, 0:part] for h in range(halves)], axis=1)
            for g in range(n // halves)
        ],
        axis=0,
    )
    extra = jnp.concatenate(
        [out[g * halves, :, part : part + LANES] for g in range(n // halves)], axis=0
    )
    return value, extra


def times_exact(x, mat, dims):
    k = x.shape[0]
    both = dot32(jnp.concatenate(split3(x), axis=0), mat, dims)
    return both[0:k] + (both[k : 2 * k] + both[2 * k : 3 * k])


def times_split(x, parts, dims):
    k = x.shape[0]
    high, mid, low = split3(x)
    mh, mm, ml = parts
    a = dot32(jnp.concatenate([high, mid, low], axis=0), mh, dims)
    b = dot32(jnp.concatenate([high, mid], axis=0), mm, dims)
    c = dot32(high, ml, dims)
    return a[0:k] + ((a[k : 2 * k] + b[0:k]) + ((a[2 * k : 3 * k] + b[k : 2 * k]) + c))


def lsqr_kernel(
    n_dp,
    n_feat,
    a_ref,
    t_ref,
    w_ref,
    sol_ref,
    ratio_ref,
    wh,
    wm,
    wl,
    u_ref,
    vec_ref,
    img_ref,
    d_stage,
    d_recv,
    d_out,
    d_stage2,
    d_recv2,
    d_out2,
    f_stage,
    f_recv,
    f_out,
    f_stage2,
    f_recv2,
    small_dp,
    small_feat,
    dp_sems,
    feat_sems,
):
    dp = Group("dp", n_dp)
    feat = Group("feat", n_feat)
    k, rows = t_ref.shape
    cols = a_ref.shape[1]
    f_halves = n_feat * SUB // k
    f_part = rows // f_halves
    d_part = cols // (n_dp * SUB // k)

    barrier = pltpu.get_barrier_semaphore()
    dp.greet(barrier)
    feat.greet(barrier)
    pl.semaphore_wait(barrier, n_dp + n_feat - 2)

    def preconditioned(vec):
        return times_split(vec, (wh[...], wm[...], wl[...]), NN)

    def adjoint_pre(vec):
        return times_split(vec, (wh[...], wm[...], wl[...]), NT)

    targets = t_ref[...]
    put_slices(d_stage, times_exact(targets, a_ref[...], NN), lane_partial(targets))
    total = dp.scatter_sum(d_stage, d_recv, dp_sems.at[0])
    dp.gather(total, d_out, dp_sems.at[1])
    h, m, l = split3(w_ref[...])
    wh[...] = h
    wm[...] = m
    wl[...] = l
    adj, squares = take_slices(d_out, k, d_part)
    beta_first = norm_of(squares)
    u_ref[...] = targets / beta_first

    v_raw = adjoint_pre(adj / beta_first)
    y_raw = preconditioned(v_raw)
    put_slices(f_stage, times_exact(y_raw, a_ref[...], NT), lane_partial(v_raw))
    total = feat.scatter_sum(f_stage, f_recv, feat_sems.at[0])
    feat.gather(total, f_out, feat_sems.at[1])
    image, squares = take_slices(f_out, k, f_part)
    alpha = norm_of(squares)
    v = v_raw / alpha
    w = y_raw / alpha
    rho_bar = alpha
    phi_bar = beta_first

    u_raw = image / alpha - alpha * u_ref[...]
    put_slices(d_stage2, times_exact(u_raw, a_ref[...], NN), lane_partial(u_raw))
    total = dp.scatter_sum(d_stage2, d_recv2, dp_sems.at[2])
    dp.gather(total, d_out2, dp_sems.at[3])
    adj, squares = take_slices(d_out2, k, d_part)
    beta = norm_of(squares)
    u_ref[...] = u_raw / beta
    rho = jnp.sqrt(rho_bar * rho_bar + beta * beta)
    cosine = rho_bar / rho
    sine = beta / rho
    phi = cosine * phi_bar
    phi_bar = sine * phi_bar
    coords = (phi / rho) * w
    v_raw = adjoint_pre(adj / beta) - beta * v
    y_raw = preconditioned(v_raw)

    put_slices(f_stage2, times_exact(y_raw, a_ref[...], NT), lane_partial(v_raw))
    put_slices(img_ref, u_ref[...], None)
    total = feat.scatter_sum(f_stage2, f_recv2, feat_sems.at[2])
    squares = total[:, f_part:]
    alpha = norm_of(squares)
    left = total[:, 0:f_part] / alpha - alpha * img_ref[feat.me]
    dp.gather(lane_partial(left), small_dp, dp_sems.at[4])
    norms = tree_sum([small_dp[i] for i in range(n_dp)])
    feat.gather(jnp.concatenate([norms, squares], axis=1), small_feat, feat_sems.at[3])
    groups = n_feat // f_halves
    norms = jnp.concatenate(
        [
            tree_sum([small_feat[g * f_halves + i, :, 0:LANES] for i in range(f_halves)])
            for g in range(groups)
        ],
        axis=0,
    )
    squares = jnp.concatenate([small_feat[g * f_halves, :, LANES:] for g in range(groups)], axis=0)
    alpha = norm_of(squares)
    theta = sine * alpha
    rho_bar = -cosine * alpha
    w = y_raw / alpha - (theta / rho) * w
    beta = norm_of(norms)
    rho = jnp.sqrt(rho_bar * rho_bar + beta * beta)
    cosine = rho_bar / rho
    sine = beta / rho
    phi = cosine * phi_bar
    phi_bar = sine * phi_bar
    sol_ref[...] = coords + (phi / rho) * w
    ratio_ref[...] = jnp.broadcast_to(phi_bar / beta_first, ratio_ref.shape)


def lsqr(design, targets, winv, n_dp, n_feat):
    rows, cols = design.shape
    k = targets.shape[0]
    d_wide = cols * k // (n_dp * SUB) + LANES
    f_wide = rows * k // (n_feat * SUB) + LANES
    vmem = pl.BlockSpec(memory_space=pltpu.VMEM)
    d_bufs = [
        pltpu.VMEM((n_dp, SUB, d_wide), F32),
        pltpu.VMEM((n_dp - 1, SUB, d_wide), F32),
        pltpu.VMEM((n_dp, SUB, d_wide), F32),
    ]
    f_bufs = [
        pltpu.VMEM((n_feat, SUB, f_wide), F32),
        pltpu.VMEM((n_feat - 1, SUB, f_wide), F32),
        pltpu.VMEM((n_feat, SUB, f_wide), F32),
    ]
    return pl.pallas_call(
        functools.partial(lsqr_kernel, n_dp, n_feat),
        out_shape=(
            jax.ShapeDtypeStruct((k, cols), F32),
            jax.ShapeDtypeStruct((k, LANES), F32),
        ),
        in_specs=[vmem] * 3,
        out_specs=(vmem, vmem),
        scratch_shapes=[pltpu.VMEM((cols, cols), BF16)] * 3
        + [
            pltpu.VMEM((k, rows), F32),
            pltpu.VMEM((k, cols), F32),
            pltpu.VMEM((n_feat, SUB, f_wide - LANES), F32),
        ]
        + d_bufs
        + d_bufs
        + f_bufs
        + f_bufs[:2]
        + [
            pltpu.VMEM((n_dp, SUB, LANES), F32),
            pltpu.VMEM((n_feat, SUB, 2 * LANES), F32),
            pltpu.SemaphoreType.DMA((5, 2, n_dp - 1)),
            pltpu.SemaphoreType.DMA((4, 2, n_feat - 1)),
        ],
        compiler_params=pltpu.CompilerParams(
            collective_id=0, has_side_effects=True, vmem_limit_bytes=56 * MIB
        ),
    )(design, targets, winv)


def body(n_dp, n_feat, design, sketch, targets):
    sketched = lax.psum_scatter(
        jnp.dot(sketch, design, preferred_element_type=F32),
        "dp",
        scatter_dimension=0,
        tiled=True,
    )
    local_gram = jnp.dot(
        sketched.T, sketched, precision=TOP_PRECISION, preferred_element_type=F32
    )
    winv = inverse_factor(lax.psum(local_gram, "dp"))
    sol, ratio = lsqr(design, targets, winv, n_dp, n_feat)
    return sol, ratio[:, 0]


def solution(mesh):
    return jax.shard_map(
        functools.partial(body, mesh.shape["dp"], mesh.shape["feat"]),
        mesh=mesh,
        in_specs=(P("dp", "feat"), P(None, "dp"), P(None, "dp")),
        out_specs=(P(None, "feat"), P()),
        check_vma=False,
    )
```

time: 1050 us -> 384 us (0.37)
  waiting for transfers between devices: 459 us -> 190 us
  other arithmetic: 265 us -> 0 us
  Pallas kernels: 0 us -> 156 us
  blocking collectives: 144 us -> 0 us
  matrix products: 116 us -> 18.2 us
  local copies, waits for them, and re-layouts: 35.3 us -> 4.97 us
    psum x4 -> x1, waiting for transfers between devices: 425 us -> 123 us  [body(): winv = inverse_factor(lax.psum(local_gram, 'dp'))]
    another operation x34 -> x0, other arithmetic: 256 us -> none  [the longest x30 172 us: body(): low_factor = jnp.linalg.cholesky(gram_mat)]
    pallas_call x0 -> x2, Pallas kernels: none -> 156 us  [the longest x1 105 us: lsqr(): pl.pallas_call(functools.partial(lsqr_kernel, n_dp, n_feat), out_shape=(j...]
    psum x5 -> x0, blocking collectives: 144 us -> none  [the longest x3 78.3 us: row_norm(): return jnp.sqrt(lax.psum(squares_of(vec), 'dp') + NORM_EPS)]
    another operation x89 -> x0, matrix products: 78.2 us -> none  [the longest x45 32.1 us: precondition(): lax.linalg.triangular_solve(low_factor, vec, left_side=False, lower=True)]
    reduce_scatter x1, waiting for transfers between devices: 33.5 us -> 67.4 us  [body(): lax.psum_scatter(jnp.dot(sketch, design, preferred_element_type=F32), 'dp...]
    another operation x45 -> x0, local copies, waits for them, and re-layouts: 25.9 us -> none  [the longest x25 23.3 us: adjoint_pre(): lax.linalg.triangular_solve(low_factor, vec, left_side=False, lower=True,...]
    dot_general x5 -> x1, matrix products: 31.7 us -> 11.7 us  [body(): jnp.dot(sketch, design, preferred_element_type=F32)]
  transfers between devices with their start and end apart: 5 -> 2, of which waited for: 5 -> 2; matrix products, arithmetic and copies ran while one was open for 1% -> 0% of each run, Pallas kernels for 0% -> 0%
where the time goes in v1:
time: 384 us; the launch traced here: 383 us
  waiting for transfers between devices  190 us (49%)
  Pallas kernels  156 us (41%)
  matrix products  18.2 us (5%)
  between operations  14.1 us (4%)
  local copies, waits for them, and re-layouts  4.97 us (1%)
    psum x1, waiting for transfers between devices, body(): winv = inverse_factor(lax.psum(local_gram, 'dp'))  123 us
    pallas_call x1, Pallas kernels, lsqr(): pl.pallas_call(functools.partial(lsqr_kernel, n_dp, n_feat), out_shape=(j...  105 us
    reduce_scatter x1, waiting for transfers between devices, body(): lax.psum_scatter(jnp.dot(sketch, design, preferred_element_type=F32), 'dp...  67.4 us
    pallas_call x1, Pallas kernels, inverse_factor(): pl.pallas_call(factor_kernel, out_shape=jax.ShapeDtypeStruct((size, size)...  50.6 us
    dot_general x1, matrix products, body(): jnp.dot(sketch, design, preferred_element_type=F32)  11.7 us
  transfers between devices with their start and end apart: 2, of which 2 were waited for; matrix products, arithmetic and copies ran while one was open for 0% of the time, Pallas kernels for 0%

profile of v1, /device:TPU:1, one launch (start us, length us, event | category | flops | bytes accessed | tf_op | source)
XLA Modules:
  0.0 383.4 jit_solution(10801908508634184087)
XLA Ops:
  7.2 0.0 reduce-scatter.2.cloned.1.call-start
  7.2 11.7 %fusion = f32[1536,1024]{1,0:T(8,128)} fusion(bf16[1536,2048]{1,0:T(8,128)(2,1)} %param.4, bf16[2048,1024]{1,0:T(8,128)(2,1)} %a_ref.1), kind=kOutput, calls=%fused_computation.1 | convolution fusion | flops 6442450944 | bytes 16777216 | tf_op jit(solution)/shard_map/dot_general | solution.py:432
  18.9 0.0 reduce-scatter.2.cloned.1.call-update
  18.9 0.0 all-reduce.2.cloned.1.call-start
  19.0 67.4 %reduce-scatter.2.cloned.1.call-done = f32[96,1024]{1,0:T(8,128)} async-done(((f32[1536,1024]{1,0:T(8,128)}), f32[96,1024]{1,0:T(8,128)}) %reduce-scatter.2.cloned.1.call-update) | async-done | bytes 393232 | tf_op jit(solution)/shard_map/reduce_scatter | solution.py:431
  86.4 6.5 %fusion.1 = f32[1024,1024]{1,0:T(8,128)} fusion(f32[96,1024]{1,0:T(8,128)} %reduce-scatter.2.cloned.1.call-done), kind=kOutput, calls=%fused_computation.2 | convolution fusion | flops 1207959552 | bytes 4587520 | tf_op jit(solution)/shard_map/dot_general | solution.py:437
  92.9 0.0 all-reduce.2.cloned.1.call-update
  92.9 122.8 %all-reduce.2.cloned.1.call-done.g_in = f32[1024,1024]{1,0:T(8,128)} async-done(((f32[1024,1024]{1,0:T(8,128)}), f32[1024,1024]{1,0:T(8,128)}) %all-reduce.2.cloned.1.call-update) | async-done | bytes 4194320 | tf_op jit(solution)/shard_map/psum | solution.py:440
  215.7 50.6 %shard_map.50.w_ref = f32[1024,1024]{1,0:T(8,128)S(1)} custom-call(f32[1024,1024]{1,0:T(8,128)} %all-reduce.2.cloned.1.call-done.g_in), custom_call_target="tpu_custom_call" | custom-call | tf_op jit(solution)/shard_map/pallas_call | solution.py:141
  266.3 0.0 copy-start
  266.3 1.9 copy-done
  268.2 105.3 %shard_map.51 = (f32[64,1024]{1,0:T(8,128)}, f32[64,128]{1,0:T(8,128)}) custom-call(bf16[2048,1024]{1,0:T(8,128)(2,1)} %a_ref.1, f32[64,2048]{1,0:T(8,128)} %t_ref.1, f32[1024,1024]{1,0:T(8,128)} %copy-done), custom_call_target="tpu_custom_call" | custom-call | tf_op jit(solution)/shard_map/pallas_call | solution.py:400
  373.5 1.4 slice_reduce_fusion
  374.9 1.7 copy.7
Async XLA Ops:
  7.2 79.2 %reduce-scatter.2.cloned.1.call-start = ((), (), s32[]{:S(2)}) async-start(), calls=%async_computation.1 | async-start | bytes 6684672 | tf_op jit(solution)/shard_map/reduce_scatter | solution.py:431
  18.9 196.8 %all-reduce.2.cloned.1.call-start = ((), (), s32[]{:S(2)}) async-start(), calls=%async_computation.2 | async-start | bytes 8388608 | tf_op jit(solution)/shard_map/psum | solution.py:440
  266.3 1.9 copy-start
Sparse Core Ops, SparseCore 0:
  19.0 67.2 reduce-scatter.1
  93.0 122.6 all-reduce.1

commit v2 on v1

--- a/solution.py
+++ b/solution.py
@@ -7,9 +7,7 @@
 from jax.experimental.pallas import tpu as pltpu
 from jax.sharding import PartitionSpec as P
 
-ITERS = 2
 NORM_EPS = 1e-06
-TOP_PRECISION = lax.Precision.HIGHEST
 F32 = jnp.float32
 BF16 = jnp.bfloat16
 MESH = pl.DeviceIdType.MESH
@@ -80,10 +78,10 @@
                 w[i] = w[i] - tree_sum([p[c] * splat_w[c] for c in range(SUB)])
 
 
-def factor_kernel(g_in, w_ref, g_ref, d_ref, wk_ref, x_ref, y_ref, z_ref):
+def factor(g_ref, w_ref, d_ref, wk_ref, x_ref, y_ref, z_ref, between):
     size = g_ref.shape[0]
     blocks = size // BLK
-    g_ref[...] = g_in[...]
+    depth = 6 * BLK
     w_ref[...] = jnp.zeros_like(w_ref)
 
     def step(k, carry):
@@ -94,6 +92,8 @@
 
             @pl.when(k == this)
             def _():
+                if this == 2:
+                    between()
                 lo = this * BLK
                 nxt = lo + BLK
                 wk = wk_ref[...]
@@ -127,32 +127,15 @@
                     j = nxt
                     while j < size:
                         wide = 2 * BLK if j % (2 * BLK) == 0 else BLK
-                        g_ref[j:, j : j + wide] -= dot32(x_ref[j:, :], y_ref[j : j + wide, :], NT)
+                        g_ref[j:, j : j + wide] -= dot32(
+                            x_ref[j:, 0:depth], y_ref[j : j + wide, 0:depth], NT
+                        )
                         j += wide
-                    w_ref[nxt:, 0:nxt] -= dot32(x_ref[nxt:, :], z_ref[:, 0:nxt], NN)
+                    w_ref[nxt:, 0:nxt] -= dot32(x_ref[nxt:, 0:depth], z_ref[0:depth, 0:nxt], NN)
 
         return carry
 
     lax.fori_loop(0, blocks, step, 0)
-
-
-def inverse_factor(gram):
-    size = gram.shape[0]
-    return pl.pallas_call(
-        factor_kernel,
-        out_shape=jax.ShapeDtypeStruct((size, size), F32),
-        in_specs=[pl.BlockSpec(memory_space=pltpu.VMEM)],
-        out_specs=pl.BlockSpec(memory_space=pltpu.VMEM),
-        scratch_shapes=[
-            pltpu.VMEM((size, size), F32),
-            pltpu.VMEM((BLK, BLK), F32),
-            pltpu.VMEM((BLK, BLK), F32),
-            pltpu.VMEM((size, 6 * BLK), BF16),
-            pltpu.VMEM((size, 6 * BLK), BF16),
-            pltpu.VMEM((6 * BLK, size), BF16),
-        ],
-        compiler_params=pltpu.CompilerParams(vmem_limit_bytes=48 * MIB),
-    )(gram)
 
 
 class Group:
@@ -190,21 +173,237 @@
             )
         )
 
-    def scatter_sum(self, stage, recv, sems):
+    def scatter_start(self, stage, recv, sems):
         self.each(lambda t: self.copy(stage.at[self.peer(t)], recv.at[t - 1], sems, t).start())
+
+    def scatter_finish(self, stage, recv, sems):
         self.each(lambda t: self.copy(stage.at[self.peer(t)], recv.at[t - 1], sems, t).wait())
         return tree_sum([stage[self.me]] + [recv[t] for t in range(self.n - 1)])
 
-    def gather(self, value, out, sems):
+    def scatter_sum(self, stage, recv, sems):
+        self.scatter_start(stage, recv, sems)
+        return self.scatter_finish(stage, recv, sems)
+
+    def gather_start(self, value, out, sems):
         out[self.me] = value
         self.each(lambda t: self.copy(out.at[self.me], out.at[self.me], sems, t).start())
 
+    def gather_finish(self, out, sems):
         def wait(t):
             src = self.source(t)
             self.copy(out.at[src], out.at[src], sems, t).wait_recv()
             self.copy(out.at[self.me], out.at[self.me], sems, t).wait_send()
 
         self.each(wait)
+
+    def gather(self, value, out, sems):
+        self.gather_start(value, out, sems)
+        self.gather_finish(out, sems)
+
+
+CORES = 2
+SUBS = 2
+DIST = (4, 3, -3, 2, -2, 1, -1, 0)
+PLUS = (0, 1, 3, 5)
+MINUS = (0, 2, 4, 6)
+GOT_PLUS = (1, 3, 5, 7)
+GOT_MINUS = (2, 4, 6, 7)
+
+
+class Line:
+    def __init__(self, n_dp):
+        self.zs = n_dp // CORES
+        me = lax.axis_index("dp")
+        self.z = me // CORES
+        self.c = lax.rem(me, CORES)
+
+    def to(self, hop):
+        chip = lax.rem(self.z + hop + self.zs, self.zs)
+        return {"dp": chip * CORES + self.c}
+
+    def partner(self):
+        return {"dp": self.z * CORES + (1 - self.c)}
+
+    def copy(self, src, dst, sems, at, device):
+        return pltpu.make_async_remote_copy(
+            src_ref=src,
+            dst_ref=dst,
+            send_sem=sems.at[(0, *at)],
+            recv_sem=sems.at[(1, *at)],
+            device_id=device,
+            device_id_type=MESH,
+        )
+
+
+def halves_sent(way, s, first):
+    if s == (0 if first else 3):
+        return (way,)
+    return (0, 1)
+
+
+def sketch_gram(line, ready, meanwhile, a_ref, s_ref, g_ref, p, pair, ring, gat, gpar, pair_sems, ring_sems, gat_sems, gpar_sems):
+    half = p.shape[3]
+    sub = half // SUBS
+    chunk = 2 * CORES * half
+    cols = a_ref.shape[1]
+    wide = 2 * LANES
+
+    def partial(*chunks):
+        rows = [
+            s_ref[
+                pl.ds(
+                    pl.multiple_of(lax.rem(line.z + DIST[e] + line.zs, line.zs) * chunk, 16), chunk
+                ),
+                :,
+            ]
+            for e in chunks
+        ]
+        left = jnp.concatenate(rows, axis=0)
+
+        def tile(i, carry):
+            at = pl.multiple_of(i * wide, wide)
+            prod = dot32(left, a_ref[:, pl.ds(at, wide)], NN)
+            for n, e in enumerate(chunks):
+                for d in range(2):
+                    for c in range(CORES):
+                        r = n * chunk + (d * CORES + c) * half
+                        p[e, d, c, :, pl.ds(at, wide)] = prod[r : r + half]
+            return carry
+
+        lax.fori_loop(0, cols // wide, tile, 0)
+
+    def pair_copy(e, d):
+        return line.copy(
+            p.at[e, d, 1 - line.c], pair.at[e, d], pair_sems, (e, d), line.partner()
+        )
+
+    def pair_send(*chunks):
+        for e in chunks:
+            for d in range(2):
+                pair_copy(e, d).start()
+
+    def piece(ref, q):
+        return ref.at[pl.ds(q * sub, sub), :]
+
+    def ring_copy(way, s, d, q):
+        e = (PLUS, MINUS)[way][s]
+        return line.copy(
+            piece(p.at[e, d, line.c], q),
+            piece(ring.at[way, s, d], q),
+            ring_sems,
+            (way, s, d, q),
+            line.to((1, -1)[way]),
+        )
+
+    def ring_step(s):
+        for e in sorted({PLUS[s], MINUS[s]}):
+            for d in range(2):
+                pair_copy(e, d).wait_recv()
+        for q in range(SUBS):
+            for d in range(2):
+                for way in range(2):
+                    if d not in halves_sent(way, s, True):
+                        continue
+                    e = (PLUS, MINUS)[way][s]
+                    at = pl.ds(q * sub, sub)
+                    value = p[e, d, line.c, at, :] + pair[e, d, at, :]
+                    if s > 0 and d in halves_sent(way, s - 1, True):
+                        ring_copy(way, s - 1, d, q).wait_recv()
+                        value = value + ring[way, s - 1, d, at, :]
+                    p[e, d, line.c, at, :] = value
+                    ring_copy(way, s, d, q).start()
+
+    def gat_copy(way, s, d, q):
+        src = (PLUS, MINUS)[way][s]
+        dst = (GOT_PLUS, GOT_MINUS)[way][s]
+        return line.copy(
+            piece(gat.at[src, d], q),
+            piece(gat.at[dst, d], q),
+            gat_sems,
+            (way, s, d, q),
+            line.to((1, -1)[way]),
+        )
+
+    def gpar_copy(e, d):
+        return line.copy(gat.at[e, d], gpar.at[e, d], gpar_sems, (e, d), line.partner())
+
+    def gather_step(s):
+        for q in range(SUBS):
+            for d in range(2):
+                for way in range(2):
+                    if d not in halves_sent(way, s, False):
+                        continue
+                    gat_copy(way, s, d, q).wait_recv()
+                    if s < 3 and d in halves_sent(way, s + 1, False):
+                        gat_copy(way, s + 1, d, q).start()
+                    if q == SUBS - 1:
+                        gpar_copy((GOT_PLUS, GOT_MINUS)[way][s], d).start()
+
+    partial(0)
+    ready()
+    pair_send(0)
+    partial(1, 2)
+    pair_send(1, 2)
+    ring_step(0)
+    partial(3, 4)
+    pair_send(3, 4)
+    ring_step(1)
+    partial(5, 6)
+    pair_send(5, 6)
+    ring_step(2)
+    partial(7)
+    pair_send(7)
+    g_ref[...] = jnp.zeros_like(g_ref)
+    ring_step(3)
+    meanwhile()
+    for d in range(2):
+        pair_copy(7, d).wait_recv()
+    for q in range(SUBS):
+        for d in range(2):
+            at = pl.ds(q * sub, sub)
+            value = p[7, d, line.c, at, :] + pair[7, d, at, :]
+            for way in range(2):
+                ring_copy(way, 3, d, q).wait_recv()
+                value = value + ring[way, 3, d, at, :]
+            gat[0, d, at, :] = value
+            for way in range(2):
+                gat_copy(way, 0, d, q).start()
+            if q == SUBS - 1:
+                gpar_copy(0, d).start()
+
+    def add(e, carry):
+        for step, at in ((0, 1), (1, 1), (2, 3), (3, 5)):
+
+            @pl.when(e == at)
+            def _():
+                gather_step(step)
+
+        for d in range(2):
+            gpar_copy(e, d).wait_recv()
+        rows = jnp.concatenate([gat[e, 0], gat[e, 1], gpar[e, 0], gpar[e, 1]], axis=0)
+        rh, rm, rl = split3(rows)
+        th, tm, tl = split3(rows.T)
+        for j in range(0, cols, wide):
+            high, mid, low = rh[:, j : j + wide], rm[:, j : j + wide], rl[:, j : j + wide]
+            g_ref[j:, j : j + wide] += (
+                dot32(th[j:], high, NN)
+                + (dot32(th[j:], mid, NN) + dot32(tm[j:], high, NN))
+                + (dot32(tm[j:], mid, NN) + dot32(th[j:], low, NN) + dot32(tl[j:], high, NN))
+            )
+        return carry
+
+    lax.fori_loop(0, 8, add, 0)
+    for e in range(8):
+        for d in range(2):
+            pair_copy(e, d).wait_send()
+            gpar_copy(e, d).wait_send()
+    for s in range(4):
+        for way in range(2):
+            for q in range(SUBS):
+                for d in halves_sent(way, s, True):
+                    ring_copy(way, s, d, q).wait_send()
+                for d in halves_sent(way, s, False):
+                    gat_copy(way, s, d, q).wait_send()
 
 
 def lane_partial(x):
@@ -260,19 +459,31 @@
     return a[0:k] + ((a[k : 2 * k] + b[0:k]) + ((a[2 * k : 3 * k] + b[k : 2 * k]) + c))
 
 
-def lsqr_kernel(
+def whole_kernel(
     n_dp,
     n_feat,
     a_ref,
+    s_ref,
     t_ref,
-    w_ref,
     sol_ref,
     ratio_ref,
+    p,
+    pair,
+    ring,
+    gat,
+    gpar,
+    pair_sems,
+    ring_sems,
+    gat_sems,
+    gpar_sems,
+    g_ref,
+    w_ref,
+    d_ref,
+    wk_ref,
     wh,
     wm,
     wl,
     u_ref,
-    vec_ref,
     img_ref,
     d_stage,
     d_recv,
@@ -301,8 +512,6 @@
     barrier = pltpu.get_barrier_semaphore()
     dp.greet(barrier)
     feat.greet(barrier)
-    pl.semaphore_wait(barrier, n_dp + n_feat - 2)
-
     def preconditioned(vec):
         return times_split(vec, (wh[...], wm[...], wl[...]), NN)
 
@@ -310,9 +519,25 @@
         return times_split(vec, (wh[...], wm[...], wl[...]), NT)
 
     targets = t_ref[...]
-    put_slices(d_stage, times_exact(targets, a_ref[...], NN), lane_partial(targets))
-    total = dp.scatter_sum(d_stage, d_recv, dp_sems.at[0])
-    dp.gather(total, d_out, dp_sems.at[1])
+
+    def ready():
+        pl.semaphore_wait(barrier, n_dp + n_feat - 2)
+
+    def meanwhile():
+        put_slices(d_stage, times_exact(t_ref[...], a_ref[...], NN), lane_partial(t_ref[...]))
+
+    sketch_gram(
+        Line(n_dp), ready, meanwhile, a_ref, s_ref, g_ref, p, pair, ring, gat, gpar,
+        pair_sems, ring_sems, gat_sems, gpar_sems,
+    )
+    dp.scatter_start(d_stage, d_recv, dp_sems.at[0])
+
+    def between():
+        total = dp.scatter_finish(d_stage, d_recv, dp_sems.at[0])
+        dp.gather_start(total, d_out, dp_sems.at[1])
+
+    factor(g_ref, w_ref, d_ref, wk_ref, wh, wm, wl, between)
+    dp.gather_finish(d_out, dp_sems.at[1])
     h, m, l = split3(w_ref[...])
     wh[...] = h
     wm[...] = m
@@ -381,12 +606,15 @@
     ratio_ref[...] = jnp.broadcast_to(phi_bar / beta_first, ratio_ref.shape)
 
 
-def lsqr(design, targets, winv, n_dp, n_feat):
+def whole(design, sketch, targets, n_dp, n_feat):
     rows, cols = design.shape
     k = targets.shape[0]
+    zs = n_dp // CORES
+    half = sketch.shape[0] // (2 * n_dp)
     d_wide = cols * k // (n_dp * SUB) + LANES
     f_wide = rows * k // (n_feat * SUB) + LANES
     vmem = pl.BlockSpec(memory_space=pltpu.VMEM)
+    sems = pltpu.SemaphoreType.DMA
     d_bufs = [
         pltpu.VMEM((n_dp, SUB, d_wide), F32),
         pltpu.VMEM((n_dp - 1, SUB, d_wide), F32),
@@ -398,17 +626,31 @@
         pltpu.VMEM((n_feat, SUB, f_wide), F32),
     ]
     return pl.pallas_call(
-        functools.partial(lsqr_kernel, n_dp, n_feat),
+        functools.partial(whole_kernel, n_dp, n_feat),
         out_shape=(
             jax.ShapeDtypeStruct((k, cols), F32),
             jax.ShapeDtypeStruct((k, LANES), F32),
         ),
         in_specs=[vmem] * 3,
         out_specs=(vmem, vmem),
-        scratch_shapes=[pltpu.VMEM((cols, cols), BF16)] * 3
+        scratch_shapes=[
+            pltpu.VMEM((zs, 2, CORES, half, cols), F32),
+            pltpu.VMEM((zs, 2, half, cols), F32),
+            pltpu.VMEM((2, 4, 2, half, cols), F32),
+            pltpu.VMEM((zs, 2, half, cols), F32),
+            pltpu.VMEM((zs, 2, half, cols), F32),
+            sems((2, zs, 2)),
+            sems((2, 2, 4, 2, SUBS)),
+            sems((2, 2, 4, 2, SUBS)),
+            sems((2, zs, 2)),
+            pltpu.VMEM((cols, cols), F32),
+            pltpu.VMEM((cols, cols), F32),
+            pltpu.VMEM((BLK, BLK), F32),
+            pltpu.VMEM((BLK, BLK), F32),
+        ]
+        + [pltpu.VMEM((cols, cols), BF16)] * 3
         + [
             pltpu.VMEM((k, rows), F32),
-            pltpu.VMEM((k, cols), F32),
             pltpu.VMEM((n_feat, SUB, f_wide - LANES), F32),
         ]
         + d_bufs
@@ -418,27 +660,17 @@
         + [
             pltpu.VMEM((n_dp, SUB, LANES), F32),
             pltpu.VMEM((n_feat, SUB, 2 * LANES), F32),
-            pltpu.SemaphoreType.DMA((5, 2, n_dp - 1)),
-            pltpu.SemaphoreType.DMA((4, 2, n_feat - 1)),
+            sems((5, 2, n_dp - 1)),
+            sems((4, 2, n_feat - 1)),
         ],
         compiler_params=pltpu.CompilerParams(
-            collective_id=0, has_side_effects=True, vmem_limit_bytes=56 * MIB
+            collective_id=0, has_side_effects=True, vmem_limit_bytes=62 * MIB
         ),
-    )(design, targets, winv)
+    )(design, sketch, targets)
 
 
 def body(n_dp, n_feat, design, sketch, targets):
-    sketched = lax.psum_scatter(
-        jnp.dot(sketch, design, preferred_element_type=F32),
-        "dp",
-        scatter_dimension=0,
-        tiled=True,
-    )
-    local_gram = jnp.dot(
-        sketched.T, sketched, precision=TOP_PRECISION, preferred_element_type=F32
-    )
-    winv = inverse_factor(lax.psum(local_gram, "dp"))
-    sol, ratio = lsqr(design, targets, winv, n_dp, n_feat)
+    sol, ratio = whole(design, sketch, targets, n_dp, n_feat)
     return sol, ratio[:, 0]
 
 

time: 384 us -> 212 us (0.55)
  waiting for transfers between devices: 190 us -> 0 us
  Pallas kernels: 156 us -> 208 us
  matrix products: 18.2 us -> 0 us
  between operations: 14.1 us -> 0.64 us
    psum x1 -> x0, waiting for transfers between devices: 123 us -> none  [body(): winv = inverse_factor(lax.psum(local_gram, 'dp'))]
    reduce_scatter x1 -> x0, waiting for transfers between devices: 67.4 us -> none  [body(): lax.psum_scatter(jnp.dot(sketch, design, preferred_element_type=F32), 'dp...]
    pallas_call x2 -> x1, Pallas kernels: 156 us -> 208 us  [whole(): pl.pallas_call(functools.partial(whole_kernel, n_dp, n_feat), out_shape=(...]
    dot_general x2 -> x0, matrix products: 18.2 us -> none  [the longest x1 11.7 us: body(): jnp.dot(sketch, design, preferred_element_type=F32)]
  transfers between devices with their start and end apart: 2 -> 0, of which waited for: 2 -> 0; matrix products, arithmetic and copies ran while one was open for 0% -> 0% of each run, Pallas kernels for 0% -> 0%
where the time goes in v2:
time: 212 us
  Pallas kernels  208 us (98%)
  local copies, waits for them, and re-layouts  3.05 us (1%)
    pallas_call x1, Pallas kernels, whole(): pl.pallas_call(functools.partial(whole_kernel, n_dp, n_feat), out_shape=(...  208 us

profile of v2, /device:TPU:1, one launch (start us, length us, event | category | flops | bytes accessed | tf_op | source)
XLA Modules:
  0.0 212.0 jit_solution(9470257921469872118)
XLA Ops:
  0.6 208.3 %shard_map.50 = (f32[64,1024]{1,0:T(8,128)}, f32[64,128]{1,0:T(8,128)}) custom-call(bf16[2048,1024]{1,0:T(8,128)(2,1)} %a_ref.1, bf16[1536,2048]{1,0:T(8,128)(2,1)} %s_ref.1, f32[64,2048]{1,0:T(8,128)} %t_ref.1), custom_call_target="tpu_custom_call" | custom-call | tf_op jit(solution)/shard_map/pallas_call | solution.py:628
  208.9 1.4 slice_reduce_fusion
  210.3 1.7 copy.6

commit v3 on v2

--- a/solution.py
+++ b/solution.py
@@ -17,6 +17,7 @@
 LANES = 128
 BLK = 128
 MIB = 2**20
+PARTS = 2
 
 
 def split3(x):
@@ -48,34 +49,52 @@
 
 
 def factor_block(d_ref, w_ref):
-    n = BLK // SUB
+    tiles = BLK // SUB
+    pivots = 2 * SUB
     rid = lax.broadcasted_iota(jnp.int32, (SUB, BLK), 0)
     lid = lax.broadcasted_iota(jnp.int32, (SUB, BLK), 1)
-    a = [d_ref[SUB * i : SUB * i + SUB, :] for i in range(n)]
-    w = [jnp.where(lid == rid + SUB * i, 1.0, 0.0) for i in range(n)]
-    for g in range(n):
-        cols = [lane_splat(a[g], SUB * g + c) for c in range(SUB)]
-        rows_a, rows_w, low_w = a[g], w[g], w[g]
-        inv_pivots = jnp.zeros((SUB, BLK), F32)
-        for k in range(SUB):
-            inv = 1.0 / row_splat(cols[k], k)
-            mult = jnp.where(rid == k, 0.0, cols[k]) * inv
-            for j in range(k + 1, SUB):
-                cols[j] = cols[j] - mult * row_splat(cols[j], k)
-            rows_a = rows_a - mult * row_splat(rows_a, k)
-            rows_w = rows_w - mult * row_splat(rows_w, k)
-            low_w = low_w - jnp.where(rid > k, mult, 0.0) * row_splat(low_w, k)
-            inv_pivots = jnp.where(rid == k, inv, inv_pivots)
-        rows_a = rows_a * inv_pivots
-        rows_w = rows_w * inv_pivots
-        w_ref[SUB * g : SUB * g + SUB, :] = low_w * jnp.sqrt(inv_pivots)
-        if g < n - 1:
-            splat_a = [row_splat(rows_a, c) for c in range(SUB)]
-            splat_w = [row_splat(rows_w, c) for c in range(SUB)]
-            for i in range(g + 1, n):
-                p = [lane_splat(a[i], SUB * g + c) for c in range(SUB)]
-                a[i] = a[i] - tree_sum([p[c] * splat_a[c] for c in range(SUB)])
-                w[i] = w[i] - tree_sum([p[c] * splat_w[c] for c in range(SUB)])
+    a = [d_ref[SUB * i : SUB * i + SUB, :] for i in range(tiles)]
+    w = [jnp.where(lid == rid + SUB * i, 1.0, 0.0) for i in range(tiles)]
+    for first in range(0, tiles, 2):
+        lane = SUB * first
+        cols = [[lane_splat(a[first + t], lane + c) for t in range(2)] for c in range(pivots)]
+        rows_a = [a[first], a[first + 1]]
+        rows_w = [w[first], w[first + 1]]
+        low_w = [w[first], w[first + 1]]
+        inv_pivots = [jnp.zeros((SUB, BLK), F32) for _ in range(2)]
+        pivot = row_splat(cols[0][0], 0)
+        for k in range(pivots):
+            h, r = divmod(k, SUB)
+            inv = 1.0 / pivot
+            if k + 1 < pivots:
+                h1, r1 = divmod(k + 1, SUB)
+                off = row_splat(cols[k + 1][h], r)
+                pivot = row_splat(cols[k + 1][h1], r1) - (off * off) * inv
+            mult = [
+                (jnp.where(rid == r, 0.0, cols[k][t]) if t == h else cols[k][t]) * inv
+                for t in range(2)
+            ]
+            below = [jnp.where(rid > r, mult[t], 0.0) if t == h else mult[t] for t in range(2)]
+            for j in range(k + 1, pivots):
+                line = row_splat(cols[j][h], r)
+                cols[j] = [cols[j][t] - mult[t] * line for t in range(2)]
+            line_a, line_w, line_l = (row_splat(x[h], r) for x in (rows_a, rows_w, low_w))
+            rows_a = [rows_a[t] - mult[t] * line_a for t in range(2)]
+            rows_w = [rows_w[t] - mult[t] * line_w for t in range(2)]
+            low_w = [low_w[t] - below[t] * line_l if t >= h else low_w[t] for t in range(2)]
+            inv_pivots[h] = jnp.where(rid == r, inv, inv_pivots[h])
+        for t in range(2):
+            rows_a[t] = rows_a[t] * inv_pivots[t]
+            rows_w[t] = rows_w[t] * inv_pivots[t]
+            at = lane + SUB * t
+            w_ref[at : at + SUB, :] = low_w[t] * jnp.sqrt(inv_pivots[t])
+        if first + 2 < tiles:
+            splat_a = [row_splat(rows_a[c // SUB], c % SUB) for c in range(pivots)]
+            splat_w = [row_splat(rows_w[c // SUB], c % SUB) for c in range(pivots)]
+            for i in range(first + 2, tiles):
+                p = [lane_splat(a[i], lane + c) for c in range(pivots)]
+                a[i] = a[i] - tree_sum([p[c] * splat_a[c] for c in range(pivots)])
+                w[i] = w[i] - tree_sum([p[c] * splat_w[c] for c in range(pivots)])
 
 
 def factor(g_ref, w_ref, d_ref, wk_ref, x_ref, y_ref, z_ref, between):
@@ -142,6 +161,7 @@
     def __init__(self, axis, n):
         self.axis, self.n = axis, n
         self.me = lax.axis_index(axis)
+        self.unsent = []
 
     def peer(self, t):
         return lax.rem(self.me + t, self.n)
@@ -176,8 +196,16 @@
     def scatter_start(self, stage, recv, sems):
         self.each(lambda t: self.copy(stage.at[self.peer(t)], recv.at[t - 1], sems, t).start())
 
-    def scatter_finish(self, stage, recv, sems):
-        self.each(lambda t: self.copy(stage.at[self.peer(t)], recv.at[t - 1], sems, t).wait())
+    def scatter_finish(self, stage, recv, sems, later=True):
+        self.each(lambda t: self.copy(stage.at[self.peer(t)], recv.at[t - 1], sems, t).wait_recv())
+
+        def copy(t):
+            return self.copy(stage.at[self.peer(t)], recv.at[t - 1], sems, t)
+
+        if later:
+            self.unsent.append(copy)
+        else:
+            self.each(lambda t: copy(t).wait_send())
         return tree_sum([stage[self.me]] + [recv[t] for t in range(self.n - 1)])
 
     def scatter_sum(self, stage, recv, sems):
@@ -192,9 +220,13 @@
         def wait(t):
             src = self.source(t)
             self.copy(out.at[src], out.at[src], sems, t).wait_recv()
-            self.copy(out.at[self.me], out.at[self.me], sems, t).wait_send()
 
         self.each(wait)
+        self.unsent.append(lambda t: self.copy(out.at[self.me], out.at[self.me], sems, t))
+
+    def finish_sends(self):
+        for copy in self.unsent:
+            self.each(lambda t: copy(t).wait_send())
 
     def gather(self, value, out, sems):
         self.gather_start(value, out, sems)
@@ -241,7 +273,7 @@
     return (0, 1)
 
 
-def sketch_gram(line, ready, meanwhile, a_ref, s_ref, g_ref, p, pair, ring, gat, gpar, pair_sems, ring_sems, gat_sems, gpar_sems):
+def sketch_gram(line, ready, loaded, meanwhile, a_ref, s_ref, g_ref, p, pair, ring, gat, gpar, pair_sems, ring_sems, gat_sems, gpar_sems):
     half = p.shape[3]
     sub = half // SUBS
     chunk = 2 * CORES * half
@@ -249,6 +281,8 @@
     wide = 2 * LANES
 
     def partial(*chunks):
+        for e in chunks:
+            loaded(e)
         rows = [
             s_ref[
                 pl.ds(
@@ -300,8 +334,9 @@
             for d in range(2):
                 pair_copy(e, d).wait_recv()
         for q in range(SUBS):
-            for d in range(2):
+            for turn in range(2):
                 for way in range(2):
+                    d = (1 - turn, turn)[way]
                     if d not in halves_sent(way, s, True):
                         continue
                     e = (PLUS, MINUS)[way][s]
@@ -342,12 +377,12 @@
     partial(0)
     ready()
     pair_send(0)
+    ring_step(0)
     partial(1, 2)
     pair_send(1, 2)
-    ring_step(0)
+    ring_step(1)
     partial(3, 4)
     pair_send(3, 4)
-    ring_step(1)
     partial(5, 6)
     pair_send(5, 6)
     ring_step(2)
@@ -372,7 +407,7 @@
                 gpar_copy(0, d).start()
 
     def add(e, carry):
-        for step, at in ((0, 1), (1, 1), (2, 3), (3, 5)):
+        for step, at in ((0, 1), (1, 1), (2, 3), (3, 7)):
 
             @pl.when(e == at)
             def _():
@@ -406,6 +441,48 @@
                     gat_copy(way, s, d, q).wait_send()
 
 
+class Chips(Group):
+    def __init__(self, line):
+        self.axis, self.n, self.me, self.c = "dp", line.zs, line.z, line.c
+        self.unsent = []
+
+    def copy(self, src, dst, sems, t):
+        return pltpu.make_async_remote_copy(
+            src_ref=src,
+            dst_ref=dst,
+            send_sem=sems.at[0, t - 1],
+            recv_sem=sems.at[1, t - 1],
+            device_id={"dp": self.peer(t) * CORES + self.c},
+            device_id_type=MESH,
+        )
+
+
+def pair_and_chips_sum(line, value, extra, halves, got, stage, recv, out, sems, pair_sems):
+    chips = Chips(line)
+    part = value.shape[1] // CORES
+    for h in range(CORES):
+        halves[h, :, 0:part] = value[:, h * part : (h + 1) * part]
+        halves[h, :, part:] = extra
+    to_other = line.copy(halves.at[1 - line.c], got, pair_sems, (0,), line.partner())
+    to_other.start()
+    to_other.wait_recv()
+    both = halves[line.c] + got[...]
+    for d in range(chips.n):
+        stage[d] = both[SUB * d : SUB * d + SUB]
+    total = chips.scatter_sum(stage, recv, sems.at[0])
+    chips.gather(total, out.at[line.c], sems.at[1])
+    back = line.copy(out.at[line.c], out.at[line.c], pair_sems, (1,), line.partner())
+    back.start()
+    back.wait()
+    to_other.wait_send()
+    chips.finish_sends()
+    rows = value.shape[0]
+    total = jnp.concatenate(
+        [out[h].reshape(rows, part + LANES)[:, 0:part] for h in range(CORES)], axis=1
+    )
+    return total, out[0].reshape(rows, part + LANES)[:, part:]
+
+
 def lane_partial(x):
     return tree_sum(
         [x[:, i : i + LANES] * x[:, i : i + LANES] for i in range(0, x.shape[1], LANES)]
@@ -437,10 +514,15 @@
         ],
         axis=0,
     )
-    extra = jnp.concatenate(
+    return value
+
+
+def take_extra(out, k, part):
+    n = out.shape[0]
+    halves = n * SUB // k
+    return jnp.concatenate(
         [out[g * halves, :, part : part + LANES] for g in range(n // halves)], axis=0
     )
-    return value, extra
 
 
 def times_exact(x, mat, dims):
@@ -462,11 +544,14 @@
 def whole_kernel(
     n_dp,
     n_feat,
-    a_ref,
-    s_ref,
+    a_hbm,
+    s_hbm,
     t_ref,
     sol_ref,
     ratio_ref,
+    a_ref,
+    s_ref,
+    load_sems,
     p,
     pair,
     ring,
@@ -488,26 +573,56 @@
     d_stage,
     d_recv,
     d_out,
+    d_halves,
+    d_got,
     d_stage2,
     d_recv2,
     d_out2,
     f_stage,
     f_recv,
     f_out,
+    f_stage_b,
+    f_recv_b,
+    f_out_b,
     f_stage2,
     f_recv2,
+    f_stage2_b,
+    f_recv2_b,
     small_dp,
     small_feat,
     dp_sems,
     feat_sems,
+    chip_sems,
+    chip_pair_sems,
 ):
     dp = Group("dp", n_dp)
     feat = Group("feat", n_feat)
     k, rows = t_ref.shape
     cols = a_ref.shape[1]
     f_halves = n_feat * SUB // k
-    f_part = rows // f_halves
+    part_rows = rows // PARTS
+    f_part = part_rows // f_halves
     d_part = cols // (n_dp * SUB // k)
+
+    line = Line(n_dp)
+    chunk = s_ref.shape[0] // line.zs
+
+    def load(e):
+        at = pl.ds(
+            pl.multiple_of(lax.rem(line.z + DIST[e] + line.zs, line.zs) * chunk, 16), chunk
+        )
+        return pltpu.make_async_copy(s_hbm.at[at, :], s_ref.at[at, :], load_sems.at[e])
+
+    design_load = pltpu.make_async_copy(a_hbm, a_ref, load_sems.at[line.zs])
+    load(0).start()
+    design_load.start()
+    for e in range(1, line.zs):
+        load(e).start()
+
+    def loaded(e):
+        if e == 0:
+            design_load.wait()
+        load(e).wait()
 
     barrier = pltpu.get_barrier_semaphore()
     dp.greet(barrier)
@@ -527,13 +642,13 @@
         put_slices(d_stage, times_exact(t_ref[...], a_ref[...], NN), lane_partial(t_ref[...]))
 
     sketch_gram(
-        Line(n_dp), ready, meanwhile, a_ref, s_ref, g_ref, p, pair, ring, gat, gpar,
+        line, ready, loaded, meanwhile, a_ref, s_ref, g_ref, p, pair, ring, gat, gpar,
         pair_sems, ring_sems, gat_sems, gpar_sems,
     )
     dp.scatter_start(d_stage, d_recv, dp_sems.at[0])
 
     def between():
-        total = dp.scatter_finish(d_stage, d_recv, dp_sems.at[0])
+        total = dp.scatter_finish(d_stage, d_recv, dp_sems.at[0], later=False)
         dp.gather_start(total, d_out, dp_sems.at[1])
 
     factor(g_ref, w_ref, d_ref, wk_ref, wh, wm, wl, between)
@@ -542,29 +657,48 @@
     wh[...] = h
     wm[...] = m
     wl[...] = l
-    adj, squares = take_slices(d_out, k, d_part)
+    adj, squares = take_slices(d_out, k, d_part), take_extra(d_out, k, d_part)
     beta_first = norm_of(squares)
     u_ref[...] = targets / beta_first
 
     v_raw = adjoint_pre(adj / beta_first)
     y_raw = preconditioned(v_raw)
-    put_slices(f_stage, times_exact(y_raw, a_ref[...], NT), lane_partial(v_raw))
-    total = feat.scatter_sum(f_stage, f_recv, feat_sems.at[0])
-    feat.gather(total, f_out, feat_sems.at[1])
-    image, squares = take_slices(f_out, k, f_part)
+    def image_start(y, v, stages, recvs, sems):
+        for i in range(PARTS):
+            at = i * part_rows
+            image = times_exact(y, a_ref[at : at + part_rows, :], NT)
+            put_slices(stages[i], image, lane_partial(v) if i == 0 else None)
+            feat.scatter_start(stages[i], recvs[i], feat_sems.at[sems + i])
+
+    image_start(y_raw, v_raw, (f_stage, f_stage_b), (f_recv, f_recv_b), 0)
+    for i, (stage, recv, out) in enumerate(
+        ((f_stage, f_recv, f_out), (f_stage_b, f_recv_b, f_out_b))
+    ):
+        total = feat.scatter_finish(stage, recv, feat_sems.at[i])
+        feat.gather_start(total, out, feat_sems.at[PARTS + i])
+    feat.gather_finish(f_out, feat_sems.at[PARTS])
+    squares = take_extra(f_out, k, f_part)
     alpha = norm_of(squares)
     v = v_raw / alpha
     w = y_raw / alpha
     rho_bar = alpha
     phi_bar = beta_first
 
-    u_raw = image / alpha - alpha * u_ref[...]
-    put_slices(d_stage2, times_exact(u_raw, a_ref[...], NN), lane_partial(u_raw))
-    total = dp.scatter_sum(d_stage2, d_recv2, dp_sems.at[2])
-    dp.gather(total, d_out2, dp_sems.at[3])
-    adj, squares = take_slices(d_out2, k, d_part)
+    adj = jnp.zeros((k, cols), F32)
+    squares = jnp.zeros((k, LANES), F32)
+    for i, out in enumerate((f_out, f_out_b)):
+        at = i * part_rows
+        if i:
+            feat.gather_finish(out, feat_sems.at[PARTS + i])
+        part = take_slices(out, k, f_part) / alpha - alpha * u_ref[:, at : at + part_rows]
+        u_ref[:, at : at + part_rows] = part
+        adj = adj + times_exact(part, a_ref[at : at + part_rows, :], NN)
+        squares = squares + lane_partial(part)
+    adj, squares = pair_and_chips_sum(
+        line, adj, squares, d_halves, d_got, d_stage2, d_recv2, d_out2, chip_sems, chip_pair_sems
+    )
     beta = norm_of(squares)
-    u_ref[...] = u_raw / beta
+    u_ref[...] = u_ref[...] / beta
     rho = jnp.sqrt(rho_bar * rho_bar + beta * beta)
     cosine = rho_bar / rho
     sine = beta / rho
@@ -574,15 +708,18 @@
     v_raw = adjoint_pre(adj / beta) - beta * v
     y_raw = preconditioned(v_raw)
 
-    put_slices(f_stage2, times_exact(y_raw, a_ref[...], NT), lane_partial(v_raw))
-    put_slices(img_ref, u_ref[...], None)
-    total = feat.scatter_sum(f_stage2, f_recv2, feat_sems.at[2])
+    image_start(y_raw, v_raw, (f_stage2, f_stage2_b), (f_recv2, f_recv2_b), 2 * PARTS)
+    for i in range(PARTS):
+        put_slices(img_ref.at[i], u_ref[:, i * part_rows : (i + 1) * part_rows], None)
+    total = feat.scatter_finish(f_stage2, f_recv2, feat_sems.at[2 * PARTS])
     squares = total[:, f_part:]
     alpha = norm_of(squares)
-    left = total[:, 0:f_part] / alpha - alpha * img_ref[feat.me]
-    dp.gather(lane_partial(left), small_dp, dp_sems.at[4])
+    left = lane_partial(total[:, 0:f_part] / alpha - alpha * img_ref[0, feat.me])
+    total = feat.scatter_finish(f_stage2_b, f_recv2_b, feat_sems.at[2 * PARTS + 1])
+    left = left + lane_partial(total / alpha - alpha * img_ref[1, feat.me])
+    dp.gather(left, small_dp, dp_sems.at[2])
     norms = tree_sum([small_dp[i] for i in range(n_dp)])
-    feat.gather(jnp.concatenate([norms, squares], axis=1), small_feat, feat_sems.at[3])
+    feat.gather(jnp.concatenate([norms, squares], axis=1), small_feat, feat_sems.at[3 * PARTS])
     groups = n_feat // f_halves
     norms = jnp.concatenate(
         [
@@ -604,6 +741,8 @@
     phi_bar = sine * phi_bar
     sol_ref[...] = coords + (phi / rho) * w
     ratio_ref[...] = jnp.broadcast_to(phi_bar / beta_first, ratio_ref.shape)
+    dp.finish_sends()
+    feat.finish_sends()
 
 
 def whole(design, sketch, targets, n_dp, n_feat):
@@ -612,7 +751,7 @@
     zs = n_dp // CORES
     half = sketch.shape[0] // (2 * n_dp)
     d_wide = cols * k // (n_dp * SUB) + LANES
-    f_wide = rows * k // (n_feat * SUB) + LANES
+    f_part = rows * k // (n_feat * SUB * PARTS)
     vmem = pl.BlockSpec(memory_space=pltpu.VMEM)
     sems = pltpu.SemaphoreType.DMA
     d_bufs = [
@@ -620,20 +759,26 @@
         pltpu.VMEM((n_dp - 1, SUB, d_wide), F32),
         pltpu.VMEM((n_dp, SUB, d_wide), F32),
     ]
-    f_bufs = [
-        pltpu.VMEM((n_feat, SUB, f_wide), F32),
-        pltpu.VMEM((n_feat - 1, SUB, f_wide), F32),
-        pltpu.VMEM((n_feat, SUB, f_wide), F32),
-    ]
+    f_bufs, f_bufs_b = (
+        [
+            pltpu.VMEM((n_feat, SUB, wide), F32),
+            pltpu.VMEM((n_feat - 1, SUB, wide), F32),
+            pltpu.VMEM((n_feat, SUB, wide), F32),
+        ]
+        for wide in (f_part + LANES, f_part)
+    )
     return pl.pallas_call(
         functools.partial(whole_kernel, n_dp, n_feat),
         out_shape=(
             jax.ShapeDtypeStruct((k, cols), F32),
             jax.ShapeDtypeStruct((k, LANES), F32),
         ),
-        in_specs=[vmem] * 3,
+        in_specs=[pl.BlockSpec(memory_space=pl.ANY)] * 2 + [vmem],
         out_specs=(vmem, vmem),
         scratch_shapes=[
+            pltpu.VMEM(design.shape, BF16),
+            pltpu.VMEM(sketch.shape, BF16),
+            sems((zs + 1,)),
             pltpu.VMEM((zs, 2, CORES, half, cols), F32),
             pltpu.VMEM((zs, 2, half, cols), F32),
             pltpu.VMEM((2, 4, 2, half, cols), F32),
@@ -651,17 +796,27 @@
         + [pltpu.VMEM((cols, cols), BF16)] * 3
         + [
             pltpu.VMEM((k, rows), F32),
-            pltpu.VMEM((n_feat, SUB, f_wide - LANES), F32),
+            pltpu.VMEM((PARTS, n_feat, SUB, f_part), F32),
         ]
         + d_bufs
-        + d_bufs
+        + [
+            pltpu.VMEM((CORES, k, cols // CORES + LANES), F32),
+            pltpu.VMEM((k, cols // CORES + LANES), F32),
+            pltpu.VMEM((zs, SUB, cols // CORES + LANES), F32),
+            pltpu.VMEM((zs - 1, SUB, cols // CORES + LANES), F32),
+            pltpu.VMEM((CORES, zs, SUB, cols // CORES + LANES), F32),
+        ]
         + f_bufs
+        + f_bufs_b
         + f_bufs[:2]
+        + f_bufs_b[:2]
         + [
             pltpu.VMEM((n_dp, SUB, LANES), F32),
             pltpu.VMEM((n_feat, SUB, 2 * LANES), F32),
-            sems((5, 2, n_dp - 1)),
-            sems((4, 2, n_feat - 1)),
+            sems((3, 2, n_dp - 1)),
+            sems((3 * PARTS + 1, 2, n_feat - 1)),
+            sems((2, 2, zs - 1)),
+            sems((2, 2)),
         ],
         compiler_params=pltpu.CompilerParams(
             collective_id=0, has_side_effects=True, vmem_limit_bytes=62 * MIB

time: 212 us -> 194 us (0.915)
  Pallas kernels: 208 us -> 191 us
    pallas_call x1, Pallas kernels: 208 us -> 191 us  [whole(): pl.pallas_call(functools.partial(whole_kernel, n_dp, n_feat), out_shape=(...]
where the time goes in v3:
time: 194 us
  Pallas kernels  191 us (98%)
  local copies, waits for them, and re-layouts  3.05 us (2%)
    pallas_call x1, Pallas kernels, whole(): pl.pallas_call(functools.partial(whole_kernel, n_dp, n_feat), out_shape=(...  191 us

profile of v3, /device:TPU:1, one launch (start us, length us, event | category | flops | bytes accessed | tf_op | source)
XLA Modules:
  0.0 194.2 jit_solution(12845417319157844000)
XLA Ops:
  0.6 190.5 %shard_map.50 = (f32[64,1024]{1,0:T(8,128)}, f32[64,128]{1,0:T(8,128)}) custom-call(bf16[2048,1024]{1,0:T(8,128)(2,1)} %a_hbm.1, bf16[1536,2048]{1,0:T(8,128)(2,1)} %s_hbm.1, f32[64,2048]{1,0:T(8,128)} %t_ref.1), custom_call_target="tpu_custom_call" | custom-call | tf_op jit(solution)/shard_map/pallas_call | solution.py:770
  191.1 1.4 slice_reduce_fusion
  192.5 1.7 copy.6
